TPU v7x, 32 devices: a whole 2x2x4 slice. The times are simulated.
32 devices in a mesh: expert: 8 (over z, core), dp: 4 (over y, x).
Axes of the slice: x: 2, y: 2, z: 4, core: 2. Of those that a mesh axis runs over, the one named last changes fastest.
Arguments:
- hidden_rows: bfloat16 [4, 4096, 768], P('dp', 'expert'), may hold values from -5 to 5
- grad_send: bfloat16 [4, 4096, 2048], P('dp', 'expert'), may hold values from -5 to 5
- row_index: int32 [8, 512], P('expert'), may hold values from 0 to 511, each once within a row
- block_expert: int32 [8, 4], P('expert'), may hold values from 0 to 1
- block_count: int32 [8, 4], P('expert'), may hold values from 1 to 128
- down_weight: bfloat16 [16, 768, 2048], P('expert', None, 'dp'), may hold values from -0.21875 to 0.21875
Outputs:
- grad_hidden: bfloat16 [4, 4096, 768], P('dp', 'expert')
- new_weight: bfloat16 [16, 768, 2048], P('expert', None, 'dp')
Inputs may be any that keep to these rules, and one draw needn't show every extreme that they name: Each row of row_index is a permutation of 0 to 511.
All inputs are finite; a program needn't handle non-finite values.
Results may differ from a plain program's by a relative error of at most 0.0085.
Values may be sent and summed in bfloat16 or wider, within the bound.
A program may use at most 128 MiB of HBM per device.

v0:
```python
import jax
import jax.numpy as jnp
from jax import lax
from jax.sharding import PartitionSpec as P

learn_rate = 0.01
epsilon = 1e-06


def partner(shard, axis, stride):
    return lax.ppermute(shard, axis, [(i, i ^ 1 << stride) for i in range(lax.axis_size(axis))])


def group_sum(statistic, bit_no, levels):
    for bit_up in range(bit_no, levels):
        statistic = statistic + partner(statistic, "dp", bit_up)
    return statistic


def adasum(vector):
    levels = lax.axis_size("dp").bit_length() - 1
    own_rank = lax.axis_index("dp")
    for halving in range(levels):
        bit_no = levels - 1 - halving
        half_width = vector.shape[2] // 2
        half_bit = own_rank >> bit_no & 1
        retained = lax.dynamic_slice_in_dim(vector, half_bit * half_width, half_width, 2)
        outgoing = lax.dynamic_slice_in_dim(vector, (1 - half_bit) * half_width, half_width, 2)
        incoming = partner(outgoing, "dp", bit_no)
        own_part = retained.astype(jnp.float32)
        other_part = incoming.astype(jnp.float32)
        inner = jnp.sum(own_part * other_part, axis=(1, 2))
        own_square = jnp.sum(own_part * own_part, axis=(1, 2))
        other_square = jnp.sum(other_part * other_part, axis=(1, 2))
        norm_a = jnp.where(half_bit == 0, own_square, other_square)
        norm_b = jnp.where(half_bit == 0, other_square, own_square)
        summed = group_sum(jnp.stack([inner, norm_a, norm_b]), bit_no, levels)
        norm_own = jnp.where(half_bit == 0, summed[1], summed[2])
        norm_other = jnp.where(half_bit == 0, summed[2], summed[1])
        coef_own = 1.0 - summed[0] / (2.0 * (norm_own + epsilon))
        coef_other = 1.0 - summed[0] / (2.0 * (norm_other + epsilon))
        vector = (
            coef_own[:, None, None] * own_part + coef_other[:, None, None] * other_part
        ).astype(jnp.bfloat16)
    return vector


def expert_gradient(hidden_local, masked, slot_expert, expert):
    selected = jnp.where(
        (slot_expert == expert)[:, None], hidden_local, jnp.zeros_like(hidden_local)
    )
    return lax.dot_general(
        selected, masked, (((0,), (0,)), ((), ())), preferred_element_type=jnp.float32
    )


def per_device(hidden_rows, grad_send, row_index, block_expert, block_count, down_weight):
    arrived = lax.all_to_all(grad_send, "expert", split_axis=1, concat_axis=1, tiled=True)
    gathered = jnp.take(arrived[0], row_index[0], axis=0)
    total_rows = gathered.shape[0]
    num_blocks = block_expert.shape[1]
    block_rows = total_rows // num_blocks
    model_width = gathered.shape[1]
    hidden_width = down_weight.shape[1]
    local_experts = down_weight.shape[0]
    position = jnp.arange(total_rows)
    live_rows = position % block_rows < jnp.repeat(
        block_count[0], block_rows, total_repeat_length=total_rows
    )
    masked = jnp.where(live_rows[:, None], gathered, jnp.zeros_like(gathered))
    blocks = masked.reshape(num_blocks, block_rows, model_width)
    experts = block_expert[0]
    slot_expert = jnp.repeat(experts, block_rows, total_repeat_length=total_rows)
    chosen = jnp.take(lax.all_gather(down_weight, "dp", axis=2, tiled=True), experts, axis=0)
    folded = jnp.einsum("nbc,nfc->nbf", blocks, chosen, preferred_element_type=jnp.float32)
    grad_hidden = folded.reshape(1, total_rows, hidden_width).astype(jnp.bfloat16)
    hidden_local = hidden_rows[0]
    gradients = [
        expert_gradient(hidden_local, masked, slot_expert, expert).astype(jnp.bfloat16)
        for expert in range(local_experts)
    ]
    merged = adasum(jnp.stack(gradients, axis=0))
    new_weight = (down_weight.astype(jnp.float32) - learn_rate * merged.astype(jnp.float32)).astype(
        jnp.bfloat16
    )
    return (grad_hidden, new_weight)


def solution(mesh):
    in_specs = (
        P("dp", "expert", None),
        P("dp", "expert", None),
        P("expert", None),
        P("expert", None),
        P("expert", None),
        P("expert", None, "dp"),
    )
    out_specs = (P("dp", "expert", None), P("expert", None, "dp"))
    return jax.shard_map(
        per_device, mesh=mesh, in_specs=in_specs, out_specs=out_specs, check_vma=False
    )
```

profile of v0, /device:TPU:0, one launch (start us, length us, event | category | flops | bytes accessed | tf_op | source)
XLA Modules:
  0.0 272.0 jit_solution(9867317603728234351)
XLA Ops:
  7.2 6.8 %copy.14 = bf16[1,512,2048]{2,0,1:T(2,128)(2,1)} copy(bf16[1,512,2048]{2,1,0:T(8,128)(2,1)} %param.13) | data formatting | bytes 4194304 | tf_op args[1]
  14.4 13.2 %reduce.3 = bf16[512,2048]{1,0:T(8,128)(2,1)S(1)} reduce(bf16[512,1,2048]{2,1,0:T(2,128)(2,1)} %bitcast.95, bf16[]{:T(256)} %broadcast.425), dimensions={1}, to_apply=%bitcast.93.reduce_sub_computation | reduce | bytes 4194306
  27.6 3.9 %reshape.368 = bf16[8,2,65536]{2,1,0:T(2,128)(2,1)} reshape(bf16[512,2048]{1,0:T(8,128)(2,1)S(1)} %reduce.3) | data formatting | bytes 4194304
  31.5 6.5 %all-to-all-start = ((bf16[8,2,65536]{2,1,0:T(2,128)(2,1)}), bf16[8,2,65536]{2,1,0:T(2,128)(2,1)S(1)}, u32[]{:S(2)}, u32[]{:S(2)}) async-start(bf16[8,2,65536]{2,1,0:T(2,128)(2,1)} %reshape.368), calls=%async_computation | async-start | bytes 4194304 | tf_op jit(solution)/shard_map/all_to_all | solution.py:58
  39.3 2.6 fusion.40
  45.1 2.6 compare_and_fusion.1
  47.7 39.3 %all-to-all-done = bf16[8,2,65536]{2,1,0:T(2,128)(2,1)S(1)} async-done(((bf16[8,2,65536]{2,1,0:T(2,128)(2,1)}), bf16[8,2,65536]{2,1,0:T(2,128)(2,1)S(1)}, u32[]{:S(2)}, u32[]{:S(2)}) %all-to-all-start) | async-done | bytes 2097184 | tf_op jit(solution)/shard_map/all_to_all | solution.py:58
  87.0 4.4 %reshape.369 = bf16[512,1,2048]{2,1,0:T(2,128)(2,1)} reshape(bf16[8,2,65536]{2,1,0:T(2,128)(2,1)S(1)} %all-to-all-done) | data formatting | bytes 4194304
  91.4 3.5 %copy.13 = bf16[1,512,2048]{2,1,0:T(8,128)(2,1)S(1)} copy(bf16[1,512,2048]{2,0,1:T(2,128)(2,1)} %bitcast.96) | data formatting | bytes 4194304
  94.9 3.3 %gather_fusion = bf16[512,2048]{1,0:T(8,128)(2,1)} fusion(bf16[512,2048]{1,0:T(8,128)(2,1)S(1)} %bitcast.94, s32[1024]{0:T(1024)S(1)} %pad_clamp_fusion.1), kind=kCustom, calls=%fused_computation | custom fusion | bytes 4196352 | tf_op jit(solution)/shard_map/jit(_take)/gather | solution.py:59
  98.2 3.7 %fusion.17 = bf16[1,768,2048]{2,1,0:T(8,128)(2,1)S(1)} fusion(bf16[1,512,768]{2,1,0:T(8,128)(2,1)S(1)} %copy-done.8, pred[512]{0:T(512)(128)(4,1)S(1)} %fusion.40, bf16[512,2048]{1,0:T(8,128)(2,1)} %gather_fusion, pred[512]{0:T(512)(128)(4,1)S(1)} %get-tuple-element.48, pred[512]{0:T(512)(128)(4,1)S(1)} %fusion.32), kind=kOutput, calls=%fused_computation.38 | convolution fusion | flops 1614675968 | bytes 6030848 | tf_op jit(solution)/shard_map/dot_general | solution.py:52
  108.2 71.1 %collective-permute-done = bf16[2,768,1024]{2,1,0:T(8,128)(2,1)S(1)} collective-permute-done((bf16[2,768,1024]{2,1,0:T(8,128)(2,1)}, bf16[2,768,1024]{2,1,0:T(8,128)(2,1)S(1)}, u32[]{:S(2)}, u32[]{:S(2)}) %collective-permute-start) | collective-permute-done | bytes 3145760 | tf_op jit(solution)/shard_map/ppermute | solution.py:11
  179.2 5.4 %fusion.7 = (f32[2]{0:T(128)S(1)}, f32[2]{0:T(128)S(1)}, f32[2]{0:T(128)S(1)}, bf16[2,768,1024]{2,1,0:T(8,128)(2,1)S(1)}) fusion(bf16[2,768,1024]{2,1,0:T(8,128)(2,1)S(1)} %collective-permute-done, s32[]{:T(128)S(6)} %select_n.203, bf16[1,768,2048]{2,1,0:T(8,128)(2,1)} %copy-done.2, bf16[1,768,2048]{2,1,0:T(8,128)(2,1)} %copy-done.1), kind=kLoop, calls=%fused_computation.20 | loop fusion | flops 18874362 | bytes 12582940 | tf_op jit(solution)/shard_map/reduce_sum | solution.py:32
  185.0 3.3 %collective-permute-done.1 = f32[3,2]{1,0:T(4,128)S(1)} collective-permute-done((f32[3,2]{1,0:T(4,128)S(1)}, f32[3,2]{1,0:T(4,128)S(1)}, u32[]{:S(2)}, u32[]{:S(2)}) %collective-permute-start.1) | collective-permute-done | bytes 56 | tf_op jit(solution)/shard_map/ppermute | solution.py:11
  188.3 3.7 %fusion.6 = bf16[2,768,1024]{2,1,0:T(8,128)(2,1)S(1)} fusion(bf16[2,768,1024]{2,1,0:T(8,128)(2,1)S(1)} %get-tuple-element.29, bf16[2,768,1024]{2,1,0:T(8,128)(2,1)} %copy-done, f32[2]{0:T(128)S(1)} %get-tuple-element.35, f32[2]{0:T(128)S(1)} %get-tuple-element.34), kind=kLoop, calls=%fused_computation.19 | loop fusion | flops 9437184 | bytes 9437200 | tf_op jit(solution)/shard_map/convert_element_type | solution.py:44
  194.8 2.6 fusion.70
  197.5 31.0 %collective-permute-done.2 = bf16[2,768,512]{2,1,0:T(8,128)(2,1)} collective-permute-done((bf16[2,768,512]{2,1,0:T(8,128)(2,1)}, bf16[2,768,512]{2,1,0:T(8,128)(2,1)}, u32[]{:S(2)}, u32[]{:S(2)}) %collective-permute-start.2) | collective-permute-done | bytes 1572896 | tf_op jit(solution)/shard_map/ppermute | solution.py:11
  228.5 2.6 fusion.13
  235.2 3.3 %collective-permute-done.4 = f32[3,2]{1,0:T(4,128)S(1)} collective-permute-done((f32[3,2]{1,0:T(4,128)S(1)}, f32[3,2]{1,0:T(4,128)S(1)}, u32[]{:S(2)}, u32[]{:S(2)}) %collective-permute-start.4) | collective-permute-done | bytes 56 | tf_op jit(solution)/shard_map/ppermute | solution.py:11
  238.5 3.6 %subtract_convert_fusion = bf16[2,768,512]{2,1,0:T(8,128)(2,1)} fusion(bf16[2,768,512]{2,1,0:T(8,128)(2,1)S(1)} %copy-done.3, bf16[2,768,512]{2,1,0:T(8,128)(2,1)} %collective-permute-done.2, f32[2]{0:T(128)S(1)} %get-tuple-element.33, f32[2]{0:T(128)S(1)} %get-tuple-element.32, bf16[2,768,1024]{2,1,0:T(8,128)(2,1)S(1)} %fusion.6, s32[]{:T(128)S(6)} %select_n.213), kind=kLoop, calls=%fused_computation.37 | loop fusion | flops 8650752 | bytes 6291476 | tf_op jit(solution)/shard_map/convert_element_type | solution.py:83
  242.1 5.6 %fusion.66 = (bf16[2,768,1024]{2,1,0:T(8,128)(2,1)S(1)}, bf16[2,768,1024]{2,1,0:T(8,128)(2,1)}) fusion(bf16[2,768,2048]{2,1,0:T(8,128)(2,1)} %all-gather.2.cloned.1.call-done), kind=kLoop, calls=%fused_computation.118 | loop fusion | bytes 12582912 | tf_op jit(solution)/shard_map/jit(_take)/gather | solution.py:74
  247.7 5.5 %gather_fusion.2 = bf16[4,768,1024]{2,1,0:T(8,128)(2,1)} fusion(bf16[2,768,1024]{2,1,0:T(8,128)(2,1)} %get-tuple-element.31, s32[1024]{0:T(1024)S(1)} %pad_clamp_fusion), kind=kCustom, calls=%fused_computation.2 | custom fusion | bytes 12582928 | tf_op jit(solution)/shard_map/jit(_take)/gather | solution.py:74
  253.2 3.6 %gather_fusion.1 = bf16[4,768,1024]{2,1,0:T(8,128)(2,1)} fusion(bf16[2,768,1024]{2,1,0:T(8,128)(2,1)S(1)} %get-tuple-element.30, s32[1024]{0:T(1024)S(1)} %pad_clamp_fusion), kind=kCustom, calls=%fused_computation.1 | custom fusion | bytes 12582928 | tf_op jit(solution)/shard_map/jit(_take)/gather | solution.py:74
  256.8 8.4 %fusion.23 = bf16[4,128,768]{2,1,0:T(8,128)(2,1)} fusion(bf16[4,768,1024]{2,1,0:T(8,128)(2,1)} %gather_fusion.2, bf16[4,768,1024]{2,1,0:T(8,128)(2,1)} %gather_fusion.1, pred[4]{0:T(512)(128)(4,1)S(1)} %compare_and_fusion.2, bf16[4,128,2048]{2,1,0:T(8,128)(2,1)} %bitcast.97, pred[4,128]{1,0:T(4,128)(4,1)S(1)} %compare_and_fusion.3, ...), kind=kOutput, calls=%fused_computation.46 | convolution fusion | flops 1644560384 | bytes 15467524 | tf_op jit(solution)/shard_map/nbc,nfc->nbf/dot_general | solution.py:75
  (49 shorter events, 18.6 us)
Async XLA Ops:
  31.5 7.2 %copy-start.7 = (s32[1,4]{1,0:T(1,128)S(1)}, s32[1,4]{1,0:T(1,128)}, u32[]{:S(2)}) copy-start(s32[1,4]{1,0:T(1,128)} %param.15) | copy-start | bytes 52
  31.5 10.5 %copy-start.6 = (s32[1,4]{1,0:T(1,128)S(1)}, s32[1,4]{1,0:T(1,128)}, u32[]{:S(2)}) copy-start(s32[1,4]{1,0:T(1,128)} %param.16) | copy-start | bytes 52
  31.5 13.6 %copy-start.5 = (s32[1,512]{1,0:T(1,128)S(1)}, s32[1,512]{1,0:T(1,128)}, u32[]{:S(2)}) copy-start(s32[1,512]{1,0:T(1,128)} %param.14) | copy-start | bytes 6148
  31.5 55.5 %all-to-all-start = ((bf16[8,2,65536]{2,1,0:T(2,128)(2,1)}), bf16[8,2,65536]{2,1,0:T(2,128)(2,1)S(1)}, u32[]{:S(2)}, u32[]{:S(2)}) async-start(bf16[8,2,65536]{2,1,0:T(2,128)(2,1)} %reshape.368), calls=%async_computation | async-start | bytes 4194304 | tf_op jit(solution)/shard_map/all_to_all | solution.py:58
  37.9 204.1 %all-gather.2.cloned.1.call-start = ((), (), s32[]{:S(2)}) async-start(), calls=%async_computation.1 | async-start | bytes 7864320 | tf_op jit(solution)/shard_map/all_gather | solution.py:74
  94.9 3.3 %copy-start.8 = (bf16[1,512,768]{2,1,0:T(8,128)(2,1)S(1)}, bf16[1,512,768]{2,1,0:T(8,128)(2,1)}, u32[]{:S(2)}) copy-start(bf16[1,512,768]{2,1,0:T(8,128)(2,1)} %param.12) | copy-start | bytes 2359300
  98.2 3.8 %copy-start.4 = (bf16[512,2048]{1,0:T(8,128)(2,1)S(1)}, bf16[512,2048]{1,0:T(8,128)(2,1)}, u32[]{:S(2)}) copy-start(bf16[512,2048]{1,0:T(8,128)(2,1)} %gather_fusion) | copy-start | bytes 6291460
  101.9 2.0 copy-start.1
  104.0 2.7 copy-start.2
  106.6 72.6 %collective-permute-start = (bf16[2,768,1024]{2,1,0:T(8,128)(2,1)}, bf16[2,768,1024]{2,1,0:T(8,128)(2,1)S(1)}, u32[]{:S(2)}, u32[]{:S(2)}) collective-permute-start(bf16[2,768,1024]{2,1,0:T(8,128)(2,1)} %fusion.15), channel_id=1, source_target_pairs={{0,2},{1,3},{2,0},{3,1},{4,6},{5,7},{6,4},{7,5},{8,10},{9,11},{10,... | collective-permute-start | bytes 9437192 | tf_op jit(solution)/shard_map/ppermute | solution.py:11
  179.2 5.4 %copy-start = (bf16[2,768,1024]{2,1,0:T(8,128)(2,1)}, bf16[2,768,1024]{2,1,0:T(8,128)(2,1)S(1)}, u32[]{:S(2)}) copy-start(bf16[2,768,1024]{2,1,0:T(8,128)(2,1)S(1)} %collective-permute-done) | copy-start | bytes 9437188
  184.7 3.7 %collective-permute-start.1 = (f32[3,2]{1,0:T(4,128)S(1)}, f32[3,2]{1,0:T(4,128)S(1)}, u32[]{:S(2)}, u32[]{:S(2)}) collective-permute-start(f32[3,2]{1,0:T(4,128)S(1)} %pad_maximum_fusion), channel_id=1, source_target_pairs={{0,2},{1,3},{2,0},{3,1},{4,6},{5,7},{6,4},{7,5},{8,10},{9,11},{10,... | collective-permute-start | bytes 80 | tf_op jit(solution)/shard_map/ppermute | solution.py:11
  193.4 35.1 %collective-permute-start.2 = (bf16[2,768,512]{2,1,0:T(8,128)(2,1)}, bf16[2,768,512]{2,1,0:T(8,128)(2,1)}, u32[]{:S(2)}, u32[]{:S(2)}) collective-permute-start(bf16[2,768,512]{2,1,0:T(8,128)(2,1)} %constant_dynamic-slice_fusion), channel_id=1, source_target_pairs={{0,1},{1,0},{2,3},{3,2},{4,5},{5,4},{6,7},{7,6},{8,9},{9,8},{10,11... | collective-permute-start | bytes 4718600 | tf_op jit(solution)/shard_map/ppermute | solution.py:11
  194.8 43.6 %copy-start.3 = (bf16[2,768,512]{2,1,0:T(8,128)(2,1)S(1)}, bf16[2,768,512]{2,1,0:T(8,128)(2,1)}, u32[]{:S(2)}) copy-start(bf16[2,768,512]{2,1,0:T(8,128)(2,1)} %param.17) | copy-start | bytes 4718596
  231.1 3.7 %collective-permute-start.3 = (f32[3,2]{1,0:T(4,128)S(1)}, f32[3,2]{1,0:T(4,128)S(1)}, u32[]{:S(2)}, u32[]{:S(2)}) collective-permute-start(f32[3,2]{1,0:T(4,128)S(1)} %pad_maximum_fusion.1), channel_id=1, source_target_pairs={{0,1},{1,0},{2,3},{3,2},{4,5},{5,4},{6,7},{7,6},{8,9},{9,8},{10,11... | collective-permute-start | bytes 80 | tf_op jit(solution)/shard_map/ppermute | solution.py:11
  234.8 3.7 %collective-permute-start.4 = (f32[3,2]{1,0:T(4,128)S(1)}, f32[3,2]{1,0:T(4,128)S(1)}, u32[]{:S(2)}, u32[]{:S(2)}) collective-permute-start(f32[3,2]{1,0:T(4,128)S(1)} %fusion.63), channel_id=1, source_target_pairs={{0,2},{1,3},{2,0},{3,1},{4,6},{5,7},{6,4},{7,5},{8,10},{9,11},{10,... | collective-permute-start | bytes 80 | tf_op jit(solution)/shard_map/ppermute | solution.py:11
Sparse Core Ops, SparseCore 0:
  40.6 73.9 all-gather.1
where the time goes:
time: 273 us; the launch traced here: 272 us
  waiting for transfers between devices  150 us (55%)
  other arithmetic  41.2 us (15%)
  local copies, waits for them, and re-layouts  40 us (15%)
  between operations  14.3 us (5%)
  matrix products  14.1 us (5%)
  starting transfers between devices  12 us (4%)
    ppermute x5, waiting for transfers between devices, partner(): lax.ppermute(shard, axis, [(i, i ^ 1 << stride) for i in range(lax.axis_s...  111 us
    all_to_all x1, waiting for transfers between devices, per_device(): lax.all_to_all(grad_send, 'expert', split_axis=1, concat_axis=1, tiled=True)  39.3 us
    unnamed x23, local copies, waits for them, and re-layouts  19.3 us
    gather x3, local copies, waits for them, and re-layouts, per_device(): jnp.take(lax.all_gather(down_weight, 'dp', axis=2, tiled=True), experts,...  14.7 us
    unnamed x1, other arithmetic  13.2 us
    dot_general x1, matrix products, per_device(): jnp.einsum('nbc,nfc->nbf', blocks, chosen, preferred_element_type=jnp.flo...  8.37 us
    reduce_sum x2, other arithmetic, adasum(): inner = jnp.sum(own_part * other_part, axis=(1, 2))  7.97 us
    all_to_all x1, starting transfers between devices, per_device(): lax.all_to_all(grad_send, 'expert', split_axis=1, concat_axis=1, tiled=True)  6.46 us
  transfers between devices with their start and end apart: 7, of which 6 were waited for; matrix products, arithmetic and copies ran while one was open for 18% of the time, Pallas kernels for 0%

commit v1 on v0

v1 whole, which is shorter than its diff:
```python
import functools

import jax
import jax.numpy as jnp
from jax import lax
from jax.experimental import pallas as pl
from jax.experimental.pallas import tpu as pltpu
from jax.sharding import PartitionSpec as P

learn_rate = 0.01
epsilon = 1e-06
MESH = pl.DeviceIdType.MESH
bf16 = jnp.bfloat16
f32 = jnp.float32


def kernel(
    n_e,
    n,
    grad_ref,
    hidden_ref,
    index_ref,
    expert_ref,
    count_ref,
    w_ref,
    gh_ref,
    nw_ref,
    arrived,
    part,
    pick,
    hall,
    outp,
    inp,
    v,
    stat,
    stat_in,
    z_send,
    z_recv,
    m_send,
    m_recv,
    h_send,
    h_recv,
    p_send,
    p_recv,
    s_send,
    s_recv,
    own_sem,
):
    rows, ff = hidden_ref.shape
    cap = arrived.shape[1]
    local, _, cols = w_ref.shape
    blocks = expert_ref.shape[0]
    block = rows // blocks
    me_e, me = lax.axis_index("expert"), lax.axis_index("dp")

    def near_e(k):
        return lax.rem(me_e + k + n_e, n_e)

    def near(k):
        return lax.rem(me + k + n, n)

    barrier = pltpu.get_barrier_semaphore()
    for k in range(1, n_e):
        pl.semaphore_signal(barrier, inc=1, device_id={"expert": near_e(k)}, device_id_type=MESH)
    for k in range(1, n):
        pl.semaphore_signal(barrier, inc=1, device_id={"dp": near(k)}, device_id_type=MESH)
    own = pltpu.make_async_copy(grad_ref.at[pl.ds(me_e * cap, cap)], arrived.at[me_e], own_sem)
    own.start()
    pl.semaphore_wait(barrier, n_e + n - 2)

    order = sorted(range(1, n_e), key=lambda k: -min(k, n_e - k))
    z_copies = {}
    for k in order:
        to = near_e(k)
        z_copies[k] = pltpu.make_async_remote_copy(
            src_ref=grad_ref.at[pl.ds(to * cap, cap)],
            dst_ref=arrived.at[me_e],
            send_sem=z_send.at[k - 1],
            recv_sem=z_recv.at[k - 1],
            device_id={"expert": to},
            device_id_type=MESH,
        )
        z_copies[k].start()
    h_copies = []
    for k in range(1, n):
        copy = pltpu.make_async_remote_copy(
            src_ref=hidden_ref,
            dst_ref=hall.at[k - 1],
            send_sem=h_send.at[k - 1],
            recv_sem=h_recv.at[k - 1],
            device_id={"dp": near(k)},
            device_id_type=MESH,
        )
        copy.start()
        h_copies.append(copy)

    for b in range(blocks):
        span = pl.ds(b * block, block)
        slot = lax.broadcasted_iota(jnp.int32, (block, rows), 0)
        row = lax.broadcasted_iota(jnp.int32, (block, rows), 1)
        hit = (index_ref[span, :] == row) & (slot < count_ref[b])
        pick[span, :] = jnp.where(hit, 1.0, 0.0).astype(bf16)

    def forward(source):
        for k in range(1, n):
            to = near(k)
            pltpu.make_async_remote_copy(
                src_ref=arrived.at[source, :, pl.ds(pl.multiple_of(to * cols, cols), cols)],
                dst_ref=part.at[k, source],
                send_sem=m_send.at[k - 1],
                recv_sem=m_recv.at[k - 1],
                device_id={"dp": to},
                device_id_type=MESH,
            ).start()

    own.wait()
    forward(me_e)
    for k in [1] + [k for k in order if k != 1]:
        z_copies[k].wait_recv()
        forward(near_e(-k))

    def slots(k):
        flat = part[k].reshape(rows, cols)
        return jnp.dot(pick[...], flat, preferred_element_type=f32).astype(bf16)

    def folded(k, b):
        return lax.dot_general(
            part_slots[k, pl.ds(b * block, block), :],
            w_ref[expert_ref[b]],
            (((1,), (1,)), ((), ())),
            preferred_element_type=f32,
        )

    part_slots = v["slots"]
    vec = v["vec"]

    p_copies = []
    for k in range(1, n):
        whole = pltpu.make_async_remote_copy(
            src_ref=part.at[k],
            dst_ref=part.at[k],
            send_sem=m_send.at[k - 1],
            recv_sem=m_recv.at[k - 1],
            device_id={"dp": near(k)},
            device_id_type=MESH,
        )
        whole.wait_recv()
        part_slots[k] = slots(k)
        for b in range(blocks):
            outp[k - 1, pl.ds(b * block, block), :] = folded(k, b).astype(bf16)
        copy = pltpu.make_async_remote_copy(
            src_ref=outp.at[k - 1],
            dst_ref=inp.at[k - 1],
            send_sem=p_send.at[k - 1],
            recv_sem=p_recv.at[k - 1],
            device_id={"dp": near(-k)},
            device_id_type=MESH,
        )
        copy.start()
        p_copies.append(copy)
    for s in range(n_e):
        part[0, s] = arrived[s, :, pl.ds(pl.multiple_of(me * cols, cols), cols)]
    part_slots[0] = slots(0)

    def gradient(k, hidden):
        for e in range(local):
            pieces = [
                jnp.where(expert_ref[b] == e, hidden[pl.ds(b * block, block), :], jnp.zeros((), bf16))
                for b in range(blocks)
            ]
            chosen = jnp.concatenate(pieces, axis=0)
            vec[near(-k), e] = lax.dot_general(
                chosen, part_slots[k], (((0,), (0,)), ((), ())), preferred_element_type=f32
            ).astype(bf16)

    gradient(0, hidden_ref)
    for k in range(1, n):
        h_copies[k - 1].wait_recv()
        gradient(k, hall.at[k - 1])

    tile = 64
    half = n // 2
    level = 0
    while half >= 1:
        count = half * local * 3
        for i in range(half):
            for e in range(local):

                def body(t, sums, i=i, e=e, half=half):
                    span = pl.ds(pl.multiple_of(t * tile, tile), tile)
                    a = vec[i, e, span, :].astype(f32)
                    b = vec[i + half, e, span, :].astype(f32)
                    return tuple(
                        total + jnp.sum(x.reshape(tile // 8, 8, cols), axis=0)
                        for total, x in zip(sums, (a * b, a * a, b * b))
                    )

                zero = jnp.zeros((8, cols), f32)
                sums = lax.fori_loop(0, ff // tile, body, (zero, zero, zero))
                for m in range(3):
                    narrow = sums[m][:, :128]
                    for c in range(1, cols // 128):
                        narrow = narrow + sums[m][:, c * 128 : (c + 1) * 128]
                    r = (i * local + e) * 3 + m
                    stat[level, pl.ds(r, 1), :] = jnp.sum(narrow, axis=0, keepdims=True)
        copies = []
        for k in range(1, n):
            copy = pltpu.make_async_remote_copy(
                src_ref=stat.at[level],
                dst_ref=stat_in.at[level, k - 1],
                send_sem=s_send.at[level, k - 1],
                recv_sem=s_recv.at[level, k - 1],
                device_id={"dp": near(k)},
                device_id_type=MESH,
            )
            copy.start()
            copies.append(copy)
        for copy in copies:
            copy.wait_recv()
        total = stat[level, :count, :]
        for k in range(1, n):
            total = total + stat_in[level, k - 1, :count, :]
        total = jnp.sum(total, axis=1, keepdims=True)
        for i in range(half):
            for e in range(local):
                r = (i * local + e) * 3
                inner, aa, bb = total[r : r + 1], total[r + 1 : r + 2], total[r + 2 : r + 3]
                coef_a = 1.0 - inner / (2.0 * (aa + epsilon))
                coef_b = 1.0 - inner / (2.0 * (bb + epsilon))

                def mix(t, _, i=i, e=e, half=half, coef_a=coef_a, coef_b=coef_b):
                    span = pl.ds(pl.multiple_of(t * tile, tile), tile)
                    a = vec[i, e, span, :].astype(f32)
                    b = vec[i + half, e, span, :].astype(f32)
                    merged = (coef_a * a + coef_b * b).astype(bf16)
                    if half > 1:
                        vec[i, e, span, :] = merged
                    else:
                        new = w_ref[e, span, :].astype(f32) - learn_rate * merged.astype(f32)
                        nw_ref[e, span, :] = new.astype(bf16)
                    return 0

                lax.fori_loop(0, ff // tile, mix, 0)
        for copy in copies:
            copy.wait_send()
        half //= 2
        level += 1

    for copy in p_copies:
        copy.wait_recv()
    for b in range(blocks):
        total = folded(0, b)
        for k in range(1, n):
            total = total + inp[k - 1, pl.ds(b * block, block), :].astype(f32)
        gh_ref[pl.ds(b * block, block), :] = total.astype(bf16)

    for k in order:
        z_copies[k].wait_send()
    for k in range(1, n):
        h_copies[k - 1].wait_send()
        p_copies[k - 1].wait_send()
        pltpu.make_async_remote_copy(
            src_ref=part.at[k],
            dst_ref=part.at[k],
            send_sem=m_send.at[k - 1],
            recv_sem=m_recv.at[k - 1],
            device_id={"dp": near(k)},
            device_id_type=MESH,
        ).wait_send()


def per_device(hidden_rows, grad_send, row_index, block_expert, block_count, down_weight):
    n_e, n = lax.axis_size("expert"), lax.axis_size("dp")
    _, rows, ff = hidden_rows.shape
    width = grad_send.shape[2]
    local, _, cols = down_weight.shape
    cap = rows // n_e
    levels = n.bit_length() - 1
    stat_rows = -(-(n // 2 * local * 3) // 8) * 8
    vmem = pl.BlockSpec(memory_space=pltpu.VMEM)
    smem = pl.BlockSpec(memory_space=pltpu.SMEM)
    dma = pltpu.SemaphoreType.DMA
    grad_hidden, new_weight = pl.pallas_call(
        functools.partial(kernel, n_e, n),
        out_shape=(
            jax.ShapeDtypeStruct((rows, ff), bf16),
            jax.ShapeDtypeStruct((local, ff, cols), bf16),
        ),
        in_specs=[pl.BlockSpec(memory_space=pl.ANY), vmem, vmem, smem, smem, vmem],
        out_specs=(vmem, vmem),
        scratch_shapes=[
            pltpu.VMEM((n_e, cap, width), bf16),
            pltpu.VMEM((n, n_e, cap, cols), bf16),
            pltpu.VMEM((rows, rows), bf16),
            pltpu.VMEM((n - 1, rows, ff), bf16),
            pltpu.VMEM((n - 1, rows, ff), bf16),
            pltpu.VMEM((n - 1, rows, ff), bf16),
            dict(
                slots=pltpu.VMEM((n, rows, cols), bf16),
                vec=pltpu.VMEM((n, local, ff, cols), bf16),
            ),
            pltpu.VMEM((levels, stat_rows, 128), f32),
            pltpu.VMEM((levels, n - 1, stat_rows, 128), f32),
            dma((n_e - 1,)),
            dma((n_e - 1,)),
            dma((n - 1,)),
            dma((n - 1,)),
            dma((n - 1,)),
            dma((n - 1,)),
            dma((n - 1,)),
            dma((n - 1,)),
            dma((levels, n - 1)),
            dma((levels, n - 1)),
            dma,
        ],
        compiler_params=pltpu.CompilerParams(
            collective_id=0, has_side_effects=True, vmem_limit_bytes=58 * 1024 * 1024
        ),
    )(
        grad_send[0],
        hidden_rows[0],
        row_index.reshape(rows, 1),
        block_expert[0],
        block_count[0],
        down_weight,
    )
    return grad_hidden[None], new_weight


def solution(mesh):
    in_specs = (
        P("dp", "expert", None),
        P("dp", "expert", None),
        P("expert", None),
        P("expert", None),
        P("expert", None),
        P("expert", None, "dp"),
    )
    out_specs = (P("dp", "expert", None), P("expert", None, "dp"))
    return jax.shard_map(
        per_device, mesh=mesh, in_specs=in_specs, out_specs=out_specs, check_vma=False
    )
```

time: 273 us -> 120 us (0.44)
  waiting for transfers between devices: 150 us -> 0 us
  Pallas kernels: 0 us -> 114 us
  other arithmetic: 41.2 us -> 0 us
  local copies, waits for them, and re-layouts: 40 us -> 4.86 us
  matrix products: 14.1 us -> 0 us
  between operations: 14.3 us -> 0.65 us
  starting transfers between devices: 12 us -> 0 us
    pallas_call x0 -> x1, Pallas kernels: none -> 114 us  [per_device(): pl.pallas_call(functools.partial(kernel, n_e, n), out_shape=(jax.ShapeDty...]
    ppermute x5 -> x0, waiting for transfers between devices: 111 us -> none  [partner(): lax.ppermute(shard, axis, [(i, i ^ 1 << stride) for i in range(lax.axis_s...]
    all_to_all x1 -> x0, waiting for transfers between devices: 39.3 us -> none  [per_device(): lax.all_to_all(grad_send, 'expert', split_axis=1, concat_axis=1, tiled=True)]
    gather x6 -> x0, local copies, waits for them, and re-layouts: 19.3 us -> none  [the longest x3 14.7 us: per_device(): jnp.take(lax.all_gather(down_weight, 'dp', axis=2, tiled=True), experts,...]
    unnamed x23 -> x4, local copies, waits for them, and re-layouts: 19.3 us -> 3.33 us
    dot_general x3 -> x0, matrix products: 14.1 us -> none  [the longest x1 8.37 us: per_device(): jnp.einsum('nbc,nfc->nbf', blocks, chosen, preferred_element_type=jnp.flo...]
    unnamed x1 -> x0, other arithmetic: 13.2 us -> none
    reduce_sum x2 -> x0, other arithmetic: 7.97 us -> none  [adasum(): inner = jnp.sum(own_part * other_part, axis=(1, 2))]
  transfers between devices with their start and end apart: 7 -> 0, of which waited for: 6 -> 0; matrix products, arithmetic and copies ran while one was open for 18% -> 0% of each run, Pallas kernels for 0% -> 0%
where the time goes in v1:
time: 120 us
  Pallas kernels  114 us (95%)
  local copies, waits for them, and re-layouts  4.86 us (4%)
    pallas_call x1, Pallas kernels, per_device(): pl.pallas_call(functools.partial(kernel, n_e, n), out_shape=(jax.ShapeDty...  114 us
    unnamed x4, local copies, waits for them, and re-layouts  3.33 us

profile of v1, /device:TPU:0, one launch (start us, length us, event | category | flops | bytes accessed | tf_op | source)
XLA Modules:
  0.0 120.0 jit_solution(857125623986303877)
XLA Ops:
  0.6 1.5 %copy.8.index_ref = s32[512,1]{1,0:T(8,128)} copy(s32[512,1]{0,1:T(1,128)} %bitcast.9) | data formatting | bytes 4096 | tf_op jit(solution)/shard_map/reshape | solution.py:322
  2.2 114.5 %shard_map.77 = (bf16[512,768]{1,0:T(8,128)(2,1)}, bf16[2,768,512]{2,1,0:T(8,128)(2,1)}) custom-call(bf16[512,2048]{1,0:T(8,128)(2,1)} %bitcast.6, bf16[512,768]{1,0:T(8,128)(2,1)} %bitcast.7, s32[512,1]{1,0:T(8,128)} %copy.8.index_ref, s32[4]{0:T(128)} %bitcast.10, s32[4]{0:T(128)} %bitcast.11, bf16[2,768,512]{2,1,0:T(8,128)(2,1)} %w_ref.1), custom_call_target="tpu_custom_call" | custom-call | tf_op jit(solution)/shard_map/pallas_call | solution.py:283
  116.7 0.0 copy-start
  116.7 2.2 %copy.11 = bf16[1,512,768]{2,1,0:T(8,128)(2,1)} copy(bf16[1,512,768]{2,1,0:T(8,128)(2,1)} %bitcast.8) | data formatting | bytes 1572864
  118.8 0.0 copy-done
  118.8 1.1 copy.12
Async XLA Ops:
  116.7 2.2 %copy-start = (bf16[2,768,512]{2,1,0:T(8,128)(2,1)S(1)}, bf16[2,768,512]{2,1,0:T(8,128)(2,1)}, u32[]{:S(2)}) copy-start(bf16[2,768,512]{2,1,0:T(8,128)(2,1)} %get-tuple-element.9) | copy-start | bytes 4718596

commit v2 on v1

--- a/solution.py
+++ b/solution.py
@@ -29,8 +29,15 @@
     part,
     pick,
     hall,
-    outp,
-    inp,
+    out_a,
+    out_b,
+    in_a,
+    in_b,
+    next_a,
+    next_b,
+    last_a,
+    last_b,
+    own_sum,
     v,
     stat,
     stat_in,
@@ -40,8 +47,12 @@
     m_recv,
     h_send,
     h_recv,
+    d_send,
+    d_recv,
     p_send,
     p_recv,
+    q_send,
+    q_recv,
     s_send,
     s_recv,
     own_sem,
@@ -56,8 +67,18 @@
     def near_e(k):
         return lax.rem(me_e + k + n_e, n_e)
 
+    n_b = 2 ** (n.bit_length() // 2)
+    n_a = n // n_b
+    me_a, me_b = lax.div(me, n_b), lax.rem(me, n_b)
+
     def near(k):
-        return lax.rem(me + k + n, n)
+        return lax.rem(me_a + k // n_b, n_a) * n_b + lax.rem(me_b + k % n_b, n_b)
+
+    def back(k):
+        return lax.rem(me_a + n_a - k // n_b, n_a) * n_b + lax.rem(me_b + n_b - k % n_b, n_b)
+
+    line_a = [d * n_b for d in range(1, n_a)]
+    line_b = list(range(1, n_b))
 
     barrier = pltpu.get_barrier_semaphore()
     for k in range(1, n_e):
@@ -81,9 +102,9 @@
             device_id_type=MESH,
         )
         z_copies[k].start()
-    h_copies = []
-    for k in range(1, n):
-        copy = pltpu.make_async_remote_copy(
+    h_copies = {}
+    for k in line_a + line_b:
+        h_copies[k] = pltpu.make_async_remote_copy(
             src_ref=hidden_ref,
             dst_ref=hall.at[k - 1],
             send_sem=h_send.at[k - 1],
@@ -91,15 +112,28 @@
             device_id={"dp": near(k)},
             device_id_type=MESH,
         )
+        h_copies[k].start()
+    d_copies = {}
+
+    def relay(k, source, to, which):
+        span = pl.ds(which * (rows // 2), rows // 2)
+        copy = pltpu.make_async_remote_copy(
+            src_ref=hall.at[source - 1, span],
+            dst_ref=hall.at[k - 1, span],
+            send_sem=d_send.at[k - 1, which],
+            recv_sem=d_recv.at[k - 1, which],
+            device_id={"dp": near(to)},
+            device_id_type=MESH,
+        )
         copy.start()
-        h_copies.append(copy)
-
+        d_copies[k, which] = copy
+
+    received = lax.broadcasted_iota(jnp.int32, (rows, rows), 0)
+    hits = jnp.where(index_ref[...] == received, 1.0, 0.0).astype(f32).T
     for b in range(blocks):
-        span = pl.ds(b * block, block)
         slot = lax.broadcasted_iota(jnp.int32, (block, rows), 0)
-        row = lax.broadcasted_iota(jnp.int32, (block, rows), 1)
-        hit = (index_ref[span, :] == row) & (slot < count_ref[b])
-        pick[span, :] = jnp.where(hit, 1.0, 0.0).astype(bf16)
+        live = jnp.where(slot < count_ref[b], hits[b * block : (b + 1) * block], 0.0)
+        pick[pl.ds(b * block, block), :] = live.astype(bf16)
 
     def forward(source):
         for k in range(1, n):
@@ -115,9 +149,18 @@
 
     own.wait()
     forward(me_e)
-    for k in [1] + [k for k in order if k != 1]:
+    for turn, k in enumerate([1] + [k for k in order if k != 1]):
         z_copies[k].wait_recv()
         forward(near_e(-k))
+        if turn == n_e // 2 - 1:
+            for k_a in line_a:
+                h_copies[k_a].wait_recv()
+                for k_b in line_b:
+                    relay(k_a + k_b, k_a, k_b, 0)
+            for k_b in line_b:
+                h_copies[k_b].wait_recv()
+                for k_a in line_a:
+                    relay(k_a + k_b, k_b, k_a, 1)
 
     def slots(k):
         flat = part[k].reshape(rows, cols)
@@ -135,32 +178,70 @@
     vec = v["vec"]
 
     p_copies = []
-    for k in range(1, n):
-        whole = pltpu.make_async_remote_copy(
-            src_ref=part.at[k],
-            dst_ref=part.at[k],
-            send_sem=m_send.at[k - 1],
-            recv_sem=m_recv.at[k - 1],
-            device_id={"dp": near(k)},
-            device_id_type=MESH,
-        )
-        whole.wait_recv()
-        part_slots[k] = slots(k)
-        for b in range(blocks):
-            outp[k - 1, pl.ds(b * block, block), :] = folded(k, b).astype(bf16)
+    half_ff = ff // 2
+
+    def send(src, dst, sems, side, d, to):
         copy = pltpu.make_async_remote_copy(
-            src_ref=outp.at[k - 1],
-            dst_ref=inp.at[k - 1],
-            send_sem=p_send.at[k - 1],
-            recv_sem=p_recv.at[k - 1],
-            device_id={"dp": near(-k)},
+            src_ref=src,
+            dst_ref=dst,
+            send_sem=sems[0].at[side, d],
+            recv_sem=sems[1].at[side, d],
+            device_id={"dp": to},
             device_id_type=MESH,
         )
         copy.start()
         p_copies.append(copy)
-    for s in range(n_e):
-        part[0, s] = arrived[s, :, pl.ds(pl.multiple_of(me * cols, cols), cols)]
-    part_slots[0] = slots(0)
+        return copy
+
+    first, second = (p_send, p_recv), (q_send, q_recv)
+    stage_a, stage_b = [], []
+    made = set()
+    for k in list(range(n - 1, 0, -1)) + [0]:
+        if k:
+            pltpu.make_async_remote_copy(
+                src_ref=part.at[k],
+                dst_ref=part.at[k],
+                send_sem=m_send.at[k - 1],
+                recv_sem=m_recv.at[k - 1],
+                device_id={"dp": near(k)},
+                device_id_type=MESH,
+            ).wait_recv()
+        else:
+            for s in range(n_e):
+                part[0, s] = arrived[s, :, pl.ds(pl.multiple_of(me * cols, cols), cols)]
+        part_slots[k] = slots(k)
+        d_a, d_b = k // n_b, k % n_b
+        for b in range(blocks):
+            span = pl.ds(b * block, block)
+            value = folded(k, b)
+            if k:
+                out_a[k, span, :] = value[:, :half_ff].astype(bf16)
+                out_b[d_b * n_a + d_a, span, :] = value[:, half_ff:].astype(bf16)
+            else:
+                own_sum[span, :] = value
+        made.add(k)
+        if d_a and all(d_a * n_b + d in made for d in range(n_b)):
+            stage_a.append(
+                send(
+                    out_a.at[pl.ds(d_a * n_b, n_b)],
+                    in_a.at[d_a - 1],
+                    first,
+                    0,
+                    d_a - 1,
+                    back(d_a * n_b),
+                )
+            )
+        if d_b and all(d * n_b + d_b in made for d in range(n_a)):
+            stage_b.append(
+                send(
+                    out_b.at[pl.ds(d_b * n_a, n_a)],
+                    in_b.at[d_b - 1],
+                    first,
+                    1,
+                    d_b - 1,
+                    back(d_b),
+                )
+            )
 
     def gradient(k, hidden):
         for e in range(local):
@@ -169,14 +250,38 @@
                 for b in range(blocks)
             ]
             chosen = jnp.concatenate(pieces, axis=0)
-            vec[near(-k), e] = lax.dot_general(
+            vec[back(k), e] = lax.dot_general(
                 chosen, part_slots[k], (((0,), (0,)), ((), ())), preferred_element_type=f32
             ).astype(bf16)
 
     gradient(0, hidden_ref)
-    for k in range(1, n):
-        h_copies[k - 1].wait_recv()
+    for k in line_a + line_b:
         gradient(k, hall.at[k - 1])
+    for k_a in line_a:
+        for k_b in line_b:
+            for which in range(2):
+                d_copies[k_a + k_b, which].wait_recv()
+            gradient(k_a + k_b, hall.at[k_a + k_b - 1])
+
+    for copy in stage_a + stage_b:
+        copy.wait_recv()
+    p_last = []
+    for d in range(1, n_b):
+        for b in range(blocks):
+            span = pl.ds(b * block, block)
+            total = out_a[d, span, :].astype(f32)
+            for g in range(n_a - 1):
+                total = total + in_a[g, d, span, :].astype(f32)
+            next_a[d - 1, span, :] = total.astype(bf16)
+        p_last.append(send(next_a.at[d - 1], last_a.at[d - 1], second, 0, d - 1, back(d)))
+    for d in range(1, n_a):
+        for b in range(blocks):
+            span = pl.ds(b * block, block)
+            total = out_b[d, span, :].astype(f32)
+            for g in range(n_b - 1):
+                total = total + in_b[g, d, span, :].astype(f32)
+            next_b[d - 1, span, :] = total.astype(bf16)
+        p_last.append(send(next_b.at[d - 1], last_b.at[d - 1], second, 1, d - 1, back(d * n_b)))
 
     tile = 64
     half = n // 2
@@ -246,19 +351,28 @@
         half //= 2
         level += 1
 
-    for copy in p_copies:
+    for copy in p_last:
         copy.wait_recv()
     for b in range(blocks):
-        total = folded(0, b)
-        for k in range(1, n):
-            total = total + inp[k - 1, pl.ds(b * block, block), :].astype(f32)
-        gh_ref[pl.ds(b * block, block), :] = total.astype(bf16)
+        span = pl.ds(b * block, block)
+        total = own_sum[span, :half_ff]
+        for g in range(n_a - 1):
+            total = total + in_a[g, 0, span, :].astype(f32)
+        for g in range(n_b - 1):
+            total = total + last_a[g, span, :].astype(f32)
+        gh_ref[span, :half_ff] = total.astype(bf16)
+        total = own_sum[span, half_ff:]
+        for g in range(n_b - 1):
+            total = total + in_b[g, 0, span, :].astype(f32)
+        for g in range(n_a - 1):
+            total = total + last_b[g, span, :].astype(f32)
+        gh_ref[span, half_ff:] = total.astype(bf16)
 
     for k in order:
         z_copies[k].wait_send()
+    for copy in list(h_copies.values()) + list(d_copies.values()) + p_copies:
+        copy.wait_send()
     for k in range(1, n):
-        h_copies[k - 1].wait_send()
-        p_copies[k - 1].wait_send()
         pltpu.make_async_remote_copy(
             src_ref=part.at[k],
             dst_ref=part.at[k],
@@ -276,6 +390,8 @@
     local, _, cols = down_weight.shape
     cap = rows // n_e
     levels = n.bit_length() - 1
+    n_b = 2 ** (n.bit_length() // 2)
+    n_a = n // n_b
     stat_rows = -(-(n // 2 * local * 3) // 8) * 8
     vmem = pl.BlockSpec(memory_space=pltpu.VMEM)
     smem = pl.BlockSpec(memory_space=pltpu.SMEM)
@@ -293,8 +409,15 @@
             pltpu.VMEM((n, n_e, cap, cols), bf16),
             pltpu.VMEM((rows, rows), bf16),
             pltpu.VMEM((n - 1, rows, ff), bf16),
-            pltpu.VMEM((n - 1, rows, ff), bf16),
-            pltpu.VMEM((n - 1, rows, ff), bf16),
+            pltpu.VMEM((n, rows, ff // 2), bf16),
+            pltpu.VMEM((n, rows, ff // 2), bf16),
+            pltpu.VMEM((n_a - 1, n_b, rows, ff // 2), bf16),
+            pltpu.VMEM((n_b - 1, n_a, rows, ff // 2), bf16),
+            pltpu.VMEM((n_b - 1, rows, ff // 2), bf16),
+            pltpu.VMEM((n_a - 1, rows, ff // 2), bf16),
+            pltpu.VMEM((n_b - 1, rows, ff // 2), bf16),
+            pltpu.VMEM((n_a - 1, rows, ff // 2), bf16),
+            pltpu.VMEM((rows, ff), f32),
             dict(
                 slots=pltpu.VMEM((n, rows, cols), bf16),
                 vec=pltpu.VMEM((n, local, ff, cols), bf16),
@@ -307,8 +430,12 @@
             dma((n - 1,)),
             dma((n - 1,)),
             dma((n - 1,)),
-            dma((n - 1,)),
-            dma((n - 1,)),
+            dma((n - 1, 2)),
+            dma((n - 1, 2)),
+            dma((2, max(n_a, n_b) - 1)),
+            dma((2, max(n_a, n_b) - 1)),
+            dma((2, max(n_a, n_b) - 1)),
+            dma((2, max(n_a, n_b) - 1)),
             dma((levels, n - 1)),
             dma((levels, n - 1)),
             dma,
@@ -319,7 +446,7 @@
     )(
         grad_send[0],
         hidden_rows[0],
-        row_index.reshape(rows, 1),
+        row_index,
         block_expert[0],
         block_count[0],
         down_weight,

time: 120 us -> 114 us (0.950)
  Pallas kernels: 114 us -> 109 us
  local copies, waits for them, and re-layouts: 4.86 us -> 3.33 us
    pallas_call x1, Pallas kernels: 114 us -> 109 us  [per_device(): pl.pallas_call(functools.partial(kernel, n_e, n), out_shape=(jax.ShapeDty...]
    reshape x1 -> x0, local copies, waits for them, and re-layouts: 1.53 us -> none  [per_device(): row_index.reshape(rows, 1)]
where the time goes in v2:
time: 114 us; the launch traced here: 113 us
  Pallas kernels  109 us (96%)
  local copies, waits for them, and re-layouts  3.33 us (3%)
    pallas_call x1, Pallas kernels, per_device(): pl.pallas_call(functools.partial(kernel, n_e, n), out_shape=(jax.ShapeDty...  109 us
    unnamed x4, local copies, waits for them, and re-layouts  3.33 us

profile of v2, /device:TPU:0, one launch (start us, length us, event | category | flops | bytes accessed | tf_op | source)
XLA Modules:
  0.0 113.2 jit_solution(12000727499922676355)
XLA Ops:
  0.6 109.2 %shard_map.77 = (bf16[512,768]{1,0:T(8,128)(2,1)}, bf16[2,768,512]{2,1,0:T(8,128)(2,1)}) custom-call(bf16[512,2048]{1,0:T(8,128)(2,1)} %bitcast.5, bf16[512,768]{1,0:T(8,128)(2,1)} %bitcast.6, s32[1,512]{1,0:T(1,128)} %index_ref.1, s32[4]{0:T(128)} %bitcast.8, s32[4]{0:T(128)} %bitcast.9, bf16[2,768,512]{2,1,0:T(8,128)(2,1)} %w_ref.1), custom_call_target="tpu_custom_call" | custom-call | tf_op jit(solution)/shard_map/pallas_call | solution.py:399
  109.9 0.0 copy-start
  109.9 2.2 %copy.10 = bf16[1,512,768]{2,1,0:T(8,128)(2,1)} copy(bf16[1,512,768]{2,1,0:T(8,128)(2,1)} %bitcast.7) | data formatting | bytes 1572864
  112.1 0.0 copy-done
  112.1 1.1 %copy.11 = bf16[2,768,512]{2,1,0:T(8,128)(2,1)} copy(bf16[2,768,512]{2,1,0:T(8,128)(2,1)S(1)} %copy-done) | data formatting | bytes 3145728
Async XLA Ops:
  109.9 2.2 %copy-start = (bf16[2,768,512]{2,1,0:T(8,128)(2,1)S(1)}, bf16[2,768,512]{2,1,0:T(8,128)(2,1)}, u32[]{:S(2)}) copy-start(bf16[2,768,512]{2,1,0:T(8,128)(2,1)} %get-tuple-element.9) | copy-start | bytes 4718596

commit v3 on v2

--- a/solution.py
+++ b/solution.py
@@ -25,7 +25,7 @@
     w_ref,
     gh_ref,
     nw_ref,
-    arrived,
+    stage,
     part,
     pick,
     hall,
@@ -58,7 +58,7 @@
     own_sem,
 ):
     rows, ff = hidden_ref.shape
-    cap = arrived.shape[1]
+    cap = part.shape[2]
     local, _, cols = w_ref.shape
     blocks = expert_ref.shape[0]
     block = rows // blocks
@@ -85,23 +85,50 @@
         pl.semaphore_signal(barrier, inc=1, device_id={"expert": near_e(k)}, device_id_type=MESH)
     for k in range(1, n):
         pl.semaphore_signal(barrier, inc=1, device_id={"dp": near(k)}, device_id_type=MESH)
-    own = pltpu.make_async_copy(grad_ref.at[pl.ds(me_e * cap, cap)], arrived.at[me_e], own_sem)
+    mine = pl.ds(pl.multiple_of(me * cols, cols), cols)
+    own = pltpu.make_async_copy(grad_ref.at[me_e, :, mine], part.at[0, me_e], own_sem)
     own.start()
     pl.semaphore_wait(barrier, n_e + n - 2)
 
+    m_copies = {}
+    for k in line_a + line_b + [a + b for a in line_a for b in line_b]:
+        to = near(k)
+        m_copies[k] = pltpu.make_async_remote_copy(
+            src_ref=grad_ref.at[:, :, pl.ds(pl.multiple_of(to * cols, cols), cols)],
+            dst_ref=stage.at[k - 1],
+            send_sem=m_send.at[k - 1],
+            recv_sem=m_recv.at[k - 1],
+            device_id={"dp": to},
+            device_id_type=MESH,
+        )
+        m_copies[k].start()
+
     order = sorted(range(1, n_e), key=lambda k: -min(k, n_e - k))
-    z_copies = {}
-    for k in order:
-        to = near_e(k)
-        z_copies[k] = pltpu.make_async_remote_copy(
-            src_ref=grad_ref.at[pl.ds(to * cap, cap)],
-            dst_ref=arrived.at[me_e],
-            send_sem=z_send.at[k - 1],
-            recv_sem=z_recv.at[k - 1],
-            device_id={"expert": to},
+
+    def spread(k):
+        for j in order:
+            to = near_e(j)
+            pltpu.make_async_remote_copy(
+                src_ref=stage.at[k - 1, to] if k else grad_ref.at[to, :, mine],
+                dst_ref=part.at[k, me_e],
+                send_sem=z_send.at[k],
+                recv_sem=z_recv.at[k],
+                device_id={"expert": to},
+                device_id_type=MESH,
+            ).start()
+
+    def spread_all(k):
+        others = part.at[k, pl.ds(0, n_e - 1)]
+        return pltpu.make_async_remote_copy(
+            src_ref=others,
+            dst_ref=others,
+            send_sem=z_send.at[k],
+            recv_sem=z_recv.at[k],
+            device_id={"expert": near_e(1)},
             device_id_type=MESH,
         )
-        z_copies[k].start()
+
+    spread(0)
     h_copies = {}
     for k in line_a + line_b:
         h_copies[k] = pltpu.make_async_remote_copy(
@@ -112,7 +139,6 @@
             device_id={"dp": near(k)},
             device_id_type=MESH,
         )
-        h_copies[k].start()
     d_copies = {}
 
     def relay(k, source, to, which):
@@ -135,32 +161,23 @@
         live = jnp.where(slot < count_ref[b], hits[b * block : (b + 1) * block], 0.0)
         pick[pl.ds(b * block, block), :] = live.astype(bf16)
 
-    def forward(source):
-        for k in range(1, n):
-            to = near(k)
-            pltpu.make_async_remote_copy(
-                src_ref=arrived.at[source, :, pl.ds(pl.multiple_of(to * cols, cols), cols)],
-                dst_ref=part.at[k, source],
-                send_sem=m_send.at[k - 1],
-                recv_sem=m_recv.at[k - 1],
-                device_id={"dp": to},
-                device_id_type=MESH,
-            ).start()
-
+    for k in m_copies:
+        m_copies[k].wait_recv()
+        spread(k)
+        part[k, me_e] = stage[k - 1, me_e]
+    for k in h_copies:
+        h_copies[k].start()
     own.wait()
-    forward(me_e)
-    for turn, k in enumerate([1] + [k for k in order if k != 1]):
-        z_copies[k].wait_recv()
-        forward(near_e(-k))
-        if turn == n_e // 2 - 1:
+
+    def relay_all():
+        for k_a in line_a:
+            h_copies[k_a].wait_recv()
+            for k_b in line_b:
+                relay(k_a + k_b, k_a, k_b, 0)
+        for k_b in line_b:
+            h_copies[k_b].wait_recv()
             for k_a in line_a:
-                h_copies[k_a].wait_recv()
-                for k_b in line_b:
-                    relay(k_a + k_b, k_a, k_b, 0)
-            for k_b in line_b:
-                h_copies[k_b].wait_recv()
-                for k_a in line_a:
-                    relay(k_a + k_b, k_b, k_a, 1)
+                relay(k_a + k_b, k_b, k_a, 1)
 
     def slots(k):
         flat = part[k].reshape(rows, cols)
@@ -194,21 +211,11 @@
         return copy
 
     first, second = (p_send, p_recv), (q_send, q_recv)
-    stage_a, stage_b = [], []
-    made = set()
-    for k in list(range(n - 1, 0, -1)) + [0]:
-        if k:
-            pltpu.make_async_remote_copy(
-                src_ref=part.at[k],
-                dst_ref=part.at[k],
-                send_sem=m_send.at[k - 1],
-                recv_sem=m_recv.at[k - 1],
-                device_id={"dp": near(k)},
-                device_id_type=MESH,
-            ).wait_recv()
-        else:
-            for s in range(n_e):
-                part[0, s] = arrived[s, :, pl.ds(pl.multiple_of(me * cols, cols), cols)]
+    p_first = []
+    for turn, k in enumerate([0] + list(m_copies)):
+        if turn == n - 1:
+            relay_all()
+        spread_all(k).wait_recv()
         part_slots[k] = slots(k)
         d_a, d_b = k // n_b, k % n_b
         for b in range(blocks):
@@ -219,29 +226,12 @@
                 out_b[d_b * n_a + d_a, span, :] = value[:, half_ff:].astype(bf16)
             else:
                 own_sum[span, :] = value
-        made.add(k)
-        if d_a and all(d_a * n_b + d in made for d in range(n_b)):
-            stage_a.append(
-                send(
-                    out_a.at[pl.ds(d_a * n_b, n_b)],
-                    in_a.at[d_a - 1],
-                    first,
-                    0,
-                    d_a - 1,
-                    back(d_a * n_b),
-                )
-            )
-        if d_b and all(d * n_b + d_b in made for d in range(n_a)):
-            stage_b.append(
-                send(
-                    out_b.at[pl.ds(d_b * n_a, n_a)],
-                    in_b.at[d_b - 1],
-                    first,
-                    1,
-                    d_b - 1,
-                    back(d_b),
-                )
-            )
+        if d_a:
+            to = back(d_a * n_b)
+            p_first.append(send(out_a.at[k], in_a.at[d_a - 1, d_b], first, 0, k, to))
+        if d_b:
+            source = out_b.at[d_b * n_a + d_a]
+            p_first.append(send(source, in_b.at[d_b - 1, d_a], first, 1, k, back(d_b)))
 
     def gradient(k, hidden):
         for e in range(local):
@@ -263,7 +253,7 @@
                 d_copies[k_a + k_b, which].wait_recv()
             gradient(k_a + k_b, hall.at[k_a + k_b - 1])
 
-    for copy in stage_a + stage_b:
+    for copy in p_first:
         copy.wait_recv()
     p_last = []
     for d in range(1, n_b):
@@ -368,19 +358,13 @@
             total = total + last_b[g, span, :].astype(f32)
         gh_ref[span, half_ff:] = total.astype(bf16)
 
-    for k in order:
-        z_copies[k].wait_send()
-    for copy in list(h_copies.values()) + list(d_copies.values()) + p_copies:
+    for k in range(n):
+        spread_all(k).wait_send()
+    for group in (m_copies, h_copies, d_copies):
+        for copy in group.values():
+            copy.wait_send()
+    for copy in p_copies:
         copy.wait_send()
-    for k in range(1, n):
-        pltpu.make_async_remote_copy(
-            src_ref=part.at[k],
-            dst_ref=part.at[k],
-            send_sem=m_send.at[k - 1],
-            recv_sem=m_recv.at[k - 1],
-            device_id={"dp": near(k)},
-            device_id_type=MESH,
-        ).wait_send()
 
 
 def per_device(hidden_rows, grad_send, row_index, block_expert, block_count, down_weight):
@@ -405,7 +389,7 @@
         in_specs=[pl.BlockSpec(memory_space=pl.ANY), vmem, vmem, smem, smem, vmem],
         out_specs=(vmem, vmem),
         scratch_shapes=[
-            pltpu.VMEM((n_e, cap, width), bf16),
+            pltpu.VMEM((n - 1, n_e, cap, cols), bf16),
             pltpu.VMEM((n, n_e, cap, cols), bf16),
             pltpu.VMEM((rows, rows), bf16),
             pltpu.VMEM((n - 1, rows, ff), bf16),
@@ -424,16 +408,16 @@
             ),
             pltpu.VMEM((levels, stat_rows, 128), f32),
             pltpu.VMEM((levels, n - 1, stat_rows, 128), f32),
-            dma((n_e - 1,)),
-            dma((n_e - 1,)),
+            dma((n,)),
+            dma((n,)),
             dma((n - 1,)),
             dma((n - 1,)),
             dma((n - 1,)),
             dma((n - 1,)),
             dma((n - 1, 2)),
             dma((n - 1, 2)),
-            dma((2, max(n_a, n_b) - 1)),
-            dma((2, max(n_a, n_b) - 1)),
+            dma((2, n)),
+            dma((2, n)),
             dma((2, max(n_a, n_b) - 1)),
             dma((2, max(n_a, n_b) - 1)),
             dma((levels, n - 1)),
@@ -444,7 +428,7 @@
             collective_id=0, has_side_effects=True, vmem_limit_bytes=58 * 1024 * 1024
         ),
     )(
-        grad_send[0],
+        grad_send.reshape(n_e, cap, width),
         hidden_rows[0],
         row_index,
         block_expert[0],

time: 114 us -> 102 us (0.89)
  Pallas kernels: 109 us -> 98.1 us
    pallas_call x1, Pallas kernels: 109 us -> 98.1 us  [per_device(): pl.pallas_call(functools.partial(kernel, n_e, n), out_shape=(jax.ShapeDty...]
where the time goes in v3:
time: 102 us
  Pallas kernels  98.1 us (96%)
  local copies, waits for them, and re-layouts  3.33 us (3%)
    pallas_call x1, Pallas kernels, per_device(): pl.pallas_call(functools.partial(kernel, n_e, n), out_shape=(jax.ShapeDty...  98.1 us
    unnamed x4, local copies, waits for them, and re-layouts  3.33 us

profile of v3, /device:TPU:0, one launch (start us, length us, event | category | flops | bytes accessed | tf_op | source)
XLA Modules:
  0.0 102.1 jit_solution(11359385687911108877)
XLA Ops:
  0.6 98.1 %shard_map.77 = (bf16[512,768]{1,0:T(8,128)(2,1)}, bf16[2,768,512]{2,1,0:T(8,128)(2,1)}) custom-call(bf16[8,64,2048]{2,1,0:T(8,128)(2,1)} %bitcast.5, bf16[512,768]{1,0:T(8,128)(2,1)} %bitcast.6, s32[1,512]{1,0:T(1,128)} %index_ref.1, s32[4]{0:T(128)} %bitcast.8, s32[4]{0:T(128)} %bitcast.9, bf16[2,768,512]{2,1,0:T(8,128)(2,1)} %w_ref.1), custom_call_target="tpu_custom_call" | custom-call | tf_op jit(solution)/shard_map/pallas_call | solution.py:383
  98.7 0.0 copy-start
  98.7 2.2 %copy.10 = bf16[1,512,768]{2,1,0:T(8,128)(2,1)} copy(bf16[1,512,768]{2,1,0:T(8,128)(2,1)} %bitcast.7) | data formatting | bytes 1572864
  100.9 0.0 copy-done
  100.9 1.1 %copy.11 = bf16[2,768,512]{2,1,0:T(8,128)(2,1)} copy(bf16[2,768,512]{2,1,0:T(8,128)(2,1)S(1)} %copy-done) | data formatting | bytes 3145728
Async XLA Ops:
  98.7 2.2 %copy-start = (bf16[2,768,512]{2,1,0:T(8,128)(2,1)S(1)}, bf16[2,768,512]{2,1,0:T(8,128)(2,1)}, u32[]{:S(2)}) copy-start(bf16[2,768,512]{2,1,0:T(8,128)(2,1)} %get-tuple-element.9) | copy-start | bytes 4718596

commit v4 on v3

--- a/solution.py
+++ b/solution.py
@@ -211,10 +211,24 @@
         return copy
 
     first, second = (p_send, p_recv), (q_send, q_recv)
+    def gradient(k, hidden):
+        for e in range(local):
+            pieces = [
+                jnp.where(expert_ref[b] == e, hidden[pl.ds(b * block, block), :], jnp.zeros((), bf16))
+                for b in range(blocks)
+            ]
+            chosen = jnp.concatenate(pieces, axis=0)
+            vec[back(k), e] = lax.dot_general(
+                chosen, part_slots[k], (((0,), (0,)), ((), ())), preferred_element_type=f32
+            ).astype(bf16)
+
+    early = [k for k in line_a + line_b if k != list(m_copies)[-1]]
     p_first = []
     for turn, k in enumerate([0] + list(m_copies)):
         if turn == n - 1:
             relay_all()
+            for k_line in early:
+                gradient(k_line, hall.at[k_line - 1])
         spread_all(k).wait_recv()
         part_slots[k] = slots(k)
         d_a, d_b = k // n_b, k % n_b
@@ -226,6 +240,8 @@
                 out_b[d_b * n_a + d_a, span, :] = value[:, half_ff:].astype(bf16)
             else:
                 own_sum[span, :] = value
+        if k == 0:
+            gradient(0, hidden_ref)
         if d_a:
             to = back(d_a * n_b)
             p_first.append(send(out_a.at[k], in_a.at[d_a - 1, d_b], first, 0, k, to))
@@ -233,50 +249,18 @@
             source = out_b.at[d_b * n_a + d_a]
             p_first.append(send(source, in_b.at[d_b - 1, d_a], first, 1, k, back(d_b)))
 
-    def gradient(k, hidden):
-        for e in range(local):
-            pieces = [
-                jnp.where(expert_ref[b] == e, hidden[pl.ds(b * block, block), :], jnp.zeros((), bf16))
-                for b in range(blocks)
-            ]
-            chosen = jnp.concatenate(pieces, axis=0)
-            vec[back(k), e] = lax.dot_general(
-                chosen, part_slots[k], (((0,), (0,)), ((), ())), preferred_element_type=f32
-            ).astype(bf16)
-
-    gradient(0, hidden_ref)
     for k in line_a + line_b:
-        gradient(k, hall.at[k - 1])
+        if k not in early:
+            gradient(k, hall.at[k - 1])
     for k_a in line_a:
         for k_b in line_b:
             for which in range(2):
                 d_copies[k_a + k_b, which].wait_recv()
             gradient(k_a + k_b, hall.at[k_a + k_b - 1])
 
-    for copy in p_first:
-        copy.wait_recv()
-    p_last = []
-    for d in range(1, n_b):
-        for b in range(blocks):
-            span = pl.ds(b * block, block)
-            total = out_a[d, span, :].astype(f32)
-            for g in range(n_a - 1):
-                total = total + in_a[g, d, span, :].astype(f32)
-            next_a[d - 1, span, :] = total.astype(bf16)
-        p_last.append(send(next_a.at[d - 1], last_a.at[d - 1], second, 0, d - 1, back(d)))
-    for d in range(1, n_a):
-        for b in range(blocks):
-            span = pl.ds(b * block, block)
-            total = out_b[d, span, :].astype(f32)
-            for g in range(n_b - 1):
-                total = total + in_b[g, d, span, :].astype(f32)
-            next_b[d - 1, span, :] = total.astype(bf16)
-        p_last.append(send(next_b.at[d - 1], last_b.at[d - 1], second, 1, d - 1, back(d * n_b)))
-
     tile = 64
-    half = n // 2
-    level = 0
-    while half >= 1:
+
+    def merge(half, level):
         count = half * local * 3
         for i in range(half):
             for e in range(local):
@@ -338,8 +322,32 @@
                 lax.fori_loop(0, ff // tile, mix, 0)
         for copy in copies:
             copy.wait_send()
-        half //= 2
-        level += 1
+
+    levels = n.bit_length() - 1
+    for level in range(levels - 1):
+        merge(n >> level + 1, level)
+
+    for copy in p_first:
+        copy.wait_recv()
+    p_last = []
+    for d in range(1, n_b):
+        for b in range(blocks):
+            span = pl.ds(b * block, block)
+            total = out_a[d, span, :].astype(f32)
+            for g in range(n_a - 1):
+                total = total + in_a[g, d, span, :].astype(f32)
+            next_a[d - 1, span, :] = total.astype(bf16)
+        p_last.append(send(next_a.at[d - 1], last_a.at[d - 1], second, 0, d - 1, back(d)))
+    for d in range(1, n_a):
+        for b in range(blocks):
+            span = pl.ds(b * block, block)
+            total = out_b[d, span, :].astype(f32)
+            for g in range(n_b - 1):
+                total = total + in_b[g, d, span, :].astype(f32)
+            next_b[d - 1, span, :] = total.astype(bf16)
+        p_last.append(send(next_b.at[d - 1], last_b.at[d - 1], second, 1, d - 1, back(d * n_b)))
+
+    merge(1, levels - 1)
 
     for copy in p_last:
         copy.wait_recv()

time: 102 us -> 98.9 us (0.970)
  Pallas kernels: 98.1 us -> 94.7 us
    pallas_call x1, Pallas kernels: 98.1 us -> 94.7 us  [per_device(): pl.pallas_call(functools.partial(kernel, n_e, n), out_shape=(jax.ShapeDty...]
where the time goes in v4:
time: 98.9 us; the launch traced here: 98.7 us
  Pallas kernels  94.7 us (96%)
  local copies, waits for them, and re-layouts  3.33 us (3%)
    pallas_call x1, Pallas kernels, per_device(): pl.pallas_call(functools.partial(kernel, n_e, n), out_shape=(jax.ShapeDty...  94.7 us
    unnamed x4, local copies, waits for them, and re-layouts  3.33 us

profile of v4, /device:TPU:0, one launch (start us, length us, event | category | flops | bytes accessed | tf_op | source)
XLA Modules:
  0.0 98.7 jit_solution(6877674675292638503)
XLA Ops:
  0.6 94.7 %shard_map.77 = (bf16[512,768]{1,0:T(8,128)(2,1)}, bf16[2,768,512]{2,1,0:T(8,128)(2,1)}) custom-call(bf16[8,64,2048]{2,1,0:T(8,128)(2,1)} %bitcast.5, bf16[512,768]{1,0:T(8,128)(2,1)} %bitcast.6, s32[1,512]{1,0:T(1,128)} %index_ref.1, s32[4]{0:T(128)} %bitcast.8, s32[4]{0:T(128)} %bitcast.9, bf16[2,768,512]{2,1,0:T(8,128)(2,1)} %w_ref.1), custom_call_target="tpu_custom_call" | custom-call | tf_op jit(solution)/shard_map/pallas_call | solution.py:391
  95.4 0.0 copy-start
  95.4 2.2 %copy.10 = bf16[1,512,768]{2,1,0:T(8,128)(2,1)} copy(bf16[1,512,768]{2,1,0:T(8,128)(2,1)} %bitcast.7) | data formatting | bytes 1572864
  97.6 0.0 copy-done
  97.6 1.1 %copy.11 = bf16[2,768,512]{2,1,0:T(8,128)(2,1)} copy(bf16[2,768,512]{2,1,0:T(8,128)(2,1)S(1)} %copy-done) | data formatting | bytes 3145728
Async XLA Ops:
  95.4 2.2 %copy-start = (bf16[2,768,512]{2,1,0:T(8,128)(2,1)S(1)}, bf16[2,768,512]{2,1,0:T(8,128)(2,1)}, u32[]{:S(2)}) copy-start(bf16[2,768,512]{2,1,0:T(8,128)(2,1)} %get-tuple-element.9) | copy-start | bytes 4718596

commit v5 on v4

--- a/solution.py
+++ b/solution.py
@@ -90,24 +90,29 @@
     own.start()
     pl.semaphore_wait(barrier, n_e + n - 2)
 
+    part_e = n_e // 2
+    near_base = lax.div(me_e, part_e) * part_e
+    bases = (part_e - near_base, near_base)
+    place = me_e - near_base
+    m_order = line_a + line_b + [a + b for a in line_a for b in line_b]
     m_copies = {}
-    for k in line_a + line_b + [a + b for a in line_a for b in line_b]:
-        to = near(k)
-        m_copies[k] = pltpu.make_async_remote_copy(
-            src_ref=grad_ref.at[:, :, pl.ds(pl.multiple_of(to * cols, cols), cols)],
-            dst_ref=stage.at[k - 1],
-            send_sem=m_send.at[k - 1],
-            recv_sem=m_recv.at[k - 1],
-            device_id={"dp": to},
-            device_id_type=MESH,
-        )
-        m_copies[k].start()
-
-    order = sorted(range(1, n_e), key=lambda k: -min(k, n_e - k))
-
-    def spread(k):
-        for j in order:
-            to = near_e(j)
+    for c in range(2):
+        for k in m_order:
+            to = near(k)
+            span = pl.ds(bases[c], part_e)
+            m_copies[k, c] = pltpu.make_async_remote_copy(
+                src_ref=grad_ref.at[span, :, pl.ds(pl.multiple_of(to * cols, cols), cols)],
+                dst_ref=stage.at[k - 1, span],
+                send_sem=m_send.at[k - 1, c],
+                recv_sem=m_recv.at[k - 1, c],
+                device_id={"dp": to},
+                device_id_type=MESH,
+            )
+            m_copies[k, c].start()
+
+    def spread(k, c):
+        for j in range(c, part_e):
+            to = bases[c] + lax.rem(place + j, part_e)
             pltpu.make_async_remote_copy(
                 src_ref=stage.at[k - 1, to] if k else grad_ref.at[to, :, mine],
                 dst_ref=part.at[k, me_e],
@@ -128,7 +133,8 @@
             device_id_type=MESH,
         )
 
-    spread(0)
+    spread(0, 0)
+    spread(0, 1)
     h_copies = {}
     for k in line_a + line_b:
         h_copies[k] = pltpu.make_async_remote_copy(
@@ -161,10 +167,12 @@
         live = jnp.where(slot < count_ref[b], hits[b * block : (b + 1) * block], 0.0)
         pick[pl.ds(b * block, block), :] = live.astype(bf16)
 
-    for k in m_copies:
-        m_copies[k].wait_recv()
-        spread(k)
-        part[k, me_e] = stage[k - 1, me_e]
+    for c in range(2):
+        for k in m_order:
+            m_copies[k, c].wait_recv()
+            spread(k, c)
+            if c:
+                part[k, me_e] = stage[k - 1, me_e]
     for k in h_copies:
         h_copies[k].start()
     own.wait()
@@ -222,9 +230,9 @@
                 chosen, part_slots[k], (((0,), (0,)), ((), ())), preferred_element_type=f32
             ).astype(bf16)
 
-    early = [k for k in line_a + line_b if k != list(m_copies)[-1]]
+    early = [k for k in line_a + line_b if k != m_order[-1]]
     p_first = []
-    for turn, k in enumerate([0] + list(m_copies)):
+    for turn, k in enumerate([0] + m_order):
         if turn == n - 1:
             relay_all()
             for k_line in early:
@@ -418,8 +426,8 @@
             pltpu.VMEM((levels, n - 1, stat_rows, 128), f32),
             dma((n,)),
             dma((n,)),
-            dma((n - 1,)),
-            dma((n - 1,)),
+            dma((n - 1, 2)),
+            dma((n - 1, 2)),
             dma((n - 1,)),
             dma((n - 1,)),
             dma((n - 1, 2)),

time: 98.9 us -> 98.6 us (level)
  no operation moved by 1% of the time
where the time goes in v5:
time: 98.6 us; the launch traced here: 98.4 us
  Pallas kernels  94.4 us (96%)
  local copies, waits for them, and re-layouts  3.33 us (3%)
    pallas_call x1, Pallas kernels, per_device(): pl.pallas_call(functools.partial(kernel, n_e, n), out_shape=(jax.ShapeDty...  94.4 us
    unnamed x4, local copies, waits for them, and re-layouts  3.33 us

profile of v5, /device:TPU:0, one launch (start us, length us, event | category | flops | bytes accessed | tf_op | source)
XLA Modules:
  0.0 98.4 jit_solution(16187760546287846099)
XLA Ops:
  0.6 94.4 %shard_map.77 = (bf16[512,768]{1,0:T(8,128)(2,1)}, bf16[2,768,512]{2,1,0:T(8,128)(2,1)}) custom-call(bf16[8,64,2048]{2,1,0:T(8,128)(2,1)} %bitcast.5, bf16[512,768]{1,0:T(8,128)(2,1)} %bitcast.6, s32[1,512]{1,0:T(1,128)} %index_ref.1, s32[4]{0:T(128)} %bitcast.8, s32[4]{0:T(128)} %bitcast.9, bf16[2,768,512]{2,1,0:T(8,128)(2,1)} %w_ref.1), custom_call_target="tpu_custom_call" | custom-call | tf_op jit(solution)/shard_map/pallas_call | solution.py:399
  95.1 0.0 copy-start
  95.1 2.2 %copy.10 = bf16[1,512,768]{2,1,0:T(8,128)(2,1)} copy(bf16[1,512,768]{2,1,0:T(8,128)(2,1)} %bitcast.7) | data formatting | bytes 1572864
  97.3 0.0 copy-done
  97.3 1.1 %copy.11 = bf16[2,768,512]{2,1,0:T(8,128)(2,1)} copy(bf16[2,768,512]{2,1,0:T(8,128)(2,1)S(1)} %copy-done) | data formatting | bytes 3145728
Async XLA Ops:
  95.1 2.2 %copy-start = (bf16[2,768,512]{2,1,0:T(8,128)(2,1)S(1)}, bf16[2,768,512]{2,1,0:T(8,128)(2,1)}, u32[]{:S(2)}) copy-start(bf16[2,768,512]{2,1,0:T(8,128)(2,1)} %get-tuple-element.9) | copy-start | bytes 4718596

commit v6 on v5

--- a/solution.py
+++ b/solution.py
@@ -230,13 +230,10 @@
                 chosen, part_slots[k], (((0,), (0,)), ((), ())), preferred_element_type=f32
             ).astype(bf16)
 
-    early = [k for k in line_a + line_b if k != m_order[-1]]
     p_first = []
     for turn, k in enumerate([0] + m_order):
         if turn == n - 1:
             relay_all()
-            for k_line in early:
-                gradient(k_line, hall.at[k_line - 1])
         spread_all(k).wait_recv()
         part_slots[k] = slots(k)
         d_a, d_b = k // n_b, k % n_b
@@ -258,8 +255,7 @@
             p_first.append(send(source, in_b.at[d_b - 1, d_a], first, 1, k, back(d_b)))
 
     for k in line_a + line_b:
-        if k not in early:
-            gradient(k, hall.at[k - 1])
+        gradient(k, hall.at[k - 1])
     for k_a in line_a:
         for k_b in line_b:
             for which in range(2):

time: 98.6 us -> 98.6 us (level)
  no operation moved by 1% of the time
where the time goes in v6:
time: 98.6 us; the launch traced here: 98.4 us
  Pallas kernels  94.4 us (96%)
  local copies, waits for them, and re-layouts  3.33 us (3%)
    pallas_call x1, Pallas kernels, per_device(): pl.pallas_call(functools.partial(kernel, n_e, n), out_shape=(jax.ShapeDty...  94.4 us
    unnamed x4, local copies, waits for them, and re-layouts  3.33 us

profile of v6, /device:TPU:0, one launch (start us, length us, event | category | flops | bytes accessed | tf_op | source)
XLA Modules:
  0.0 98.4 jit_solution(6158705063268386413)
XLA Ops:
  0.6 94.4 %shard_map.77 = (bf16[512,768]{1,0:T(8,128)(2,1)}, bf16[2,768,512]{2,1,0:T(8,128)(2,1)}) custom-call(bf16[8,64,2048]{2,1,0:T(8,128)(2,1)} %bitcast.5, bf16[512,768]{1,0:T(8,128)(2,1)} %bitcast.6, s32[1,512]{1,0:T(1,128)} %index_ref.1, s32[4]{0:T(128)} %bitcast.8, s32[4]{0:T(128)} %bitcast.9, bf16[2,768,512]{2,1,0:T(8,128)(2,1)} %w_ref.1), custom_call_target="tpu_custom_call" | custom-call | tf_op jit(solution)/shard_map/pallas_call | solution.py:395
  95.1 0.0 copy-start
  95.1 2.2 %copy.10 = bf16[1,512,768]{2,1,0:T(8,128)(2,1)} copy(bf16[1,512,768]{2,1,0:T(8,128)(2,1)} %bitcast.7) | data formatting | bytes 1572864
  97.3 0.0 copy-done
  97.3 1.1 %copy.11 = bf16[2,768,512]{2,1,0:T(8,128)(2,1)} copy(bf16[2,768,512]{2,1,0:T(8,128)(2,1)S(1)} %copy-done) | data formatting | bytes 3145728
Async XLA Ops:
  95.1 2.2 %copy-start = (bf16[2,768,512]{2,1,0:T(8,128)(2,1)S(1)}, bf16[2,768,512]{2,1,0:T(8,128)(2,1)}, u32[]{:S(2)}) copy-start(bf16[2,768,512]{2,1,0:T(8,128)(2,1)} %get-tuple-element.9) | copy-start | bytes 4718596
